TPU v7x, 256 devices: a whole 4x4x8 slice. The times are simulated.
256 devices in a mesh: section: 64 (over x, z, core), head: 4 (over y).
Axes of the slice: x: 4, y: 4, z: 8, core: 2. Of those that a mesh axis runs over, the one named last changes fastest.
Arguments:
- state: bfloat16 [64, 256, 3072], P('section', None, 'head'), may hold values from -6 to 6
- modulation: float32 [64, 3, 3072], P('section'), may hold values from -3 to 3
- w_qkv: bfloat16 [64, 3072, 3, 1536], P('section', None, None, 'head'), may hold values from -0.109375 to 0.109375
- w_out: bfloat16 [64, 1536, 3072], P('section', 'head'), may hold values from -0.15625 to 0.15625
- stale_kv: bfloat16 [64, 2, 1152, 1536], P('section', None, None, 'head'), may hold values from -4 to 4
- patch_order: int32 [4], replicated, may hold values from 0 to 3, each once
- text_count: int32 [1], replicated, may hold values from 32 to 128
Outputs:
- state_out: bfloat16 [64, 256, 3072], P('section', None, 'head')
- fresh_kv: bfloat16 [64, 2, 2, 256, 1536], P('section', None, None, None, 'head')
Inputs may be any that keep to these rules, and one draw needn't show every extreme that they name: `patch_order`: each patch once.
All inputs are finite; a program needn't handle non-finite values.
Results may differ from a plain program's by a relative error of at most 0.01.
Values may be sent and summed in bfloat16 or wider, within the bound.
A program may use at most 128 MiB of HBM per device.

v0:
```python
import jax
import jax.numpy as jnp
from jax import lax
from jax.sharding import PartitionSpec as P

HEAD_DIM = 128
TICKS = 2


epsilon = 1e-06


def from_behind(value, axis, steps):
    count = lax.axis_size(axis)
    pairs = [(source, (source + steps) % count) for source in range(count)]
    return lax.ppermute(value, axis, pairs)


def modulate(full_rows, shift_row, scale_row):
    widened = full_rows.astype(jnp.float32)
    centre = jnp.mean(widened, axis=-1, keepdims=True)
    spread = jnp.mean((widened - centre) ** 2, axis=-1, keepdims=True)
    normed = (widened - centre) * lax.rsqrt(spread + epsilon) * (1.0 + scale_row) + shift_row
    return normed.astype(jnp.bfloat16)


def head_norm(columns, head_count):
    shaped = columns.reshape(columns.shape[0], head_count, HEAD_DIM)
    squares = jnp.mean(shaped * shaped, axis=-1, keepdims=True)
    return (shaped * lax.rsqrt(squares + epsilon)).astype(jnp.bfloat16)


def project(
    full_rows,
    moment,
    section_index,
    factors,
    weights,
    out_weight,
    stale_cache,
    patch_order,
    text_count,
):
    patch_rows = full_rows.shape[0]
    patches = patch_order.shape[0]
    text_rows = stale_cache.shape[1] - patches * patch_rows
    slot_index = jnp.mod(moment - section_index, patches)
    first_row = text_rows + patch_order[slot_index] * patch_rows
    zero_col = jnp.zeros((), jnp.int32)
    normed = modulate(full_rows, factors[0], factors[1])
    projected = jnp.dot(normed, weights, preferred_element_type=jnp.float32)
    inner_width = weights.shape[1] // 3
    head_count = inner_width // HEAD_DIM
    queries = head_norm(projected[:, :inner_width], head_count)
    new_keys = head_norm(projected[:, inner_width : 2 * inner_width], head_count).reshape(
        patch_rows, inner_width
    )
    new_values = projected[:, 2 * inner_width :].astype(jnp.bfloat16)
    all_keys = lax.dynamic_update_slice(stale_cache[0], new_keys, (first_row, zero_col))
    all_values = lax.dynamic_update_slice(stale_cache[1], new_values, (first_row, zero_col))
    key_count = all_keys.shape[0]
    scores = jnp.einsum(
        "phd,khd->hpk",
        queries,
        all_keys.reshape(key_count, head_count, HEAD_DIM),
        preferred_element_type=jnp.float32,
    ) * HEAD_DIM ** (-0.5)
    positions = jnp.arange(key_count)
    visible = (positions < text_count[0]) | (positions >= text_rows)
    exponent = jnp.where(visible[None, None, :], jnp.exp(scores), 0.0)
    totals = jnp.sum(exponent, axis=-1)
    mixed = jnp.einsum(
        "hpk,khd->phd",
        exponent.astype(jnp.bfloat16),
        all_values.reshape(key_count, head_count, HEAD_DIM),
        preferred_element_type=jnp.float32,
    )
    attended = (
        (mixed / jnp.transpose(totals)[:, :, None])
        .astype(jnp.bfloat16)
        .reshape(patch_rows, inner_width)
    )
    partial_value = jnp.dot(attended, out_weight, preferred_element_type=jnp.float32)
    fresh_pair = jnp.stack([new_keys, new_values])
    new_cache = jnp.stack([all_keys, all_values])
    return (partial_value, fresh_pair, new_cache)


def per_device(state, modulation, w_qkv, w_out, stale_kv, patch_order, text_count):
    section_index = lax.axis_index("section")
    head_index = lax.axis_index("head")
    factors = modulation[0]
    weights = w_qkv[0].reshape(w_qkv.shape[1], -1)
    out_weight = w_out[0]
    stale_cache = stale_kv[0]
    own_share = state[0]
    share_width = own_share.shape[1]
    fresh_list = []
    full_rows = lax.all_gather(own_share, "head", axis=1, tiled=True)
    for moment in range(TICKS):
        partial_value, fresh_pair, stale_cache = project(
            full_rows,
            moment,
            section_index,
            factors,
            weights,
            out_weight,
            stale_cache,
            patch_order,
            text_count,
        )
        summed = lax.psum(partial_value.astype(jnp.bfloat16), "head").astype(jnp.float32)
        updated = (full_rows.astype(jnp.float32) + factors[2] * summed).astype(jnp.bfloat16)
        full_rows = from_behind(updated, "section", 1)
        fresh_list.append(fresh_pair)
    result = lax.dynamic_slice_in_dim(full_rows, head_index * share_width, share_width, 1)
    return (result[None], jnp.stack(fresh_list, axis=0)[None])


def solution(mesh):
    placed = (
        P("section", None, "head"),
        P("section", None, None),
        P("section", None, None, "head"),
        P("section", "head", None),
        P("section", None, None, "head"),
        P(),
        P(),
    )
    return jax.shard_map(
        per_device,
        mesh=mesh,
        in_specs=placed,
        out_specs=(P("section", None, "head"), P("section", None, None, None, "head")),
        check_vma=False,
    )
```

profile of v0, /device:TPU:1, one launch (start us, length us, event | category | flops | bytes accessed | tf_op | source)
XLA Modules:
  0.0 277.0 jit_solution(9956343109889191630)
XLA Ops:
  10.7 2.6 fusion.59
  13.3 2.3 copy.39
  17.1 10.3 %copy.18 = bf16[1,3072,3,384]{1,3,2,0:T(8,128)(2,1)} copy(bf16[1,3072,3,384]{3,1,2,0:T(8,128)(2,1)} %param.9) | data formatting | bytes 14155776 | tf_op args[2]
  28.6 14.2 %all-gather.3.cloned.1.call-done = bf16[1,256,3072]{2,1,0:T(8,128)(2,1)} async-done(((bf16[1,256,768]{2,1,0:T(8,128)(2,1)}), bf16[1,256,3072]{2,1,0:T(8,128)(2,1)}) %all-gather.3.cloned.1.call-update) | async-done | bytes 1572880 | tf_op jit(solution)/shard_map/all_gather | solution.py:99
  42.8 1.8 convert_reduce_fusion.1
  44.6 2.0 fusion.14
  46.6 5.5 %fusion.26 = f32[256,1152]{1,0:T(8,128)S(1)} fusion(bf16[3072,1152]{0,1:T(8,128)(2,1)} %bitcast.88, bf16[1,256,3072]{2,1,0:T(8,128)(2,1)S(1)} %copy-done.1, f32[3072]{0:T(1024)S(1)} %bitcast.110, f32[3072]{0:T(1024)S(1)} %bitcast.112, f32[256]{0:T(256)S(1)} %add_rsqrt_fusion.5, f32[256]{0:T(256)S(1)} %broadcast_multiply_fusion.1), kind=kOutput, calls=%fused_computation.35 | convolution fusion | flops 1816657920 | bytes 9857024 | tf_op jit(solution)/shard_map/dot_general | solution.py:51
  53.5 1.7 copy.19
  55.3 1.9 copy.22
  59.0 1.9 copy.23
  60.9 1.9 fusion.61
  62.8 1.9 copy.20
  67.5 1.8 constant_dynamic-update-slice_fusion.2
  69.3 2.4 fusion.64
  72.4 2.2 convolution_convert_fusion.1
  74.7 55.6 %all-reduce.3.cloned.1.call-done = bf16[256,3072]{1,0:T(8,128)(2,1)} async-done(((bf16[256,3072]{1,0:T(8,128)(2,1)}), bf16[256,3072]{1,0:T(8,128)(2,1)}) %all-reduce.3.cloned.1.call-update) | async-done | bytes 1572880 | tf_op jit(solution)/shard_map/psum | solution.py:112
  130.3 3.7 %fusion.18 = bf16[256,3072]{1,0:T(8,128)(2,1)} fusion(bf16[1,256,3072]{2,1,0:T(8,128)(2,1)} %all-gather.3.cloned.1.call-done, bf16[256,3072]{1,0:T(8,128)(2,1)} %all-reduce.3.cloned.1.call-done, f32[3072]{0:T(1024)S(1)} %bitcast.108), kind=kLoop, calls=%fused_computation.27 | loop fusion | flops 3932160 | bytes 4730880 | tf_op jit(solution)/shard_map/convert_element_type | solution.py:113
  134.0 2.0 collective-permute-start
  136.6 17.0 %collective-permute-done = bf16[256,3072]{1,0:T(8,128)(2,1)} collective-permute-done((bf16[256,3072]{1,0:T(8,128)(2,1)}, bf16[256,3072]{1,0:T(8,128)(2,1)}, u32[]{:S(2)}, u32[]{:S(2)}) %collective-permute-start) | collective-permute-done | bytes 1572896 | tf_op jit(solution)/shard_map/ppermute | solution.py:16
  155.3 2.0 fusion.10
  157.3 5.9 %fusion.28 = f32[256,1152]{1,0:T(8,128)S(1)} fusion(bf16[3072,1152]{0,1:T(8,128)(2,1)} %bitcast.89, bf16[256,3072]{1,0:T(8,128)(2,1)} %collective-permute-done, f32[256]{0:T(256)S(1)} %add_rsqrt_fusion.4, f32[256]{0:T(256)S(1)} %broadcast_multiply_fusion, f32[3072]{0:T(1024)S(1)} %bitcast.111, f32[3072]{0:T(1024)S(1)} %bitcast.113), kind=kOutput, calls=%fused_computation.36 | convolution fusion | flops 1816657920 | bytes 9857024 | tf_op jit(solution)/shard_map/dot_general | solution.py:51
  166.9 1.9 copy.29
  170.6 1.9 copy.30
  172.5 2.1 fusion.60
  174.6 1.9 copy.28
  182.7 2.3 fusion.65
  185.7 2.2 convolution_convert_fusion
  187.8 57.5 %all-reduce.5.cloned.1.call-done = bf16[256,3072]{1,0:T(8,128)(2,1)} async-done(((bf16[256,3072]{1,0:T(8,128)(2,1)}), bf16[256,3072]{1,0:T(8,128)(2,1)}) %all-reduce.5.cloned.1.call-update) | async-done | bytes 1572880 | tf_op jit(solution)/shard_map/psum | solution.py:112
  245.4 3.6 %fusion.19 = bf16[256,3072]{1,0:T(8,128)(2,1)} fusion(bf16[256,3072]{1,0:T(8,128)(2,1)} %collective-permute-done, bf16[256,3072]{1,0:T(8,128)(2,1)} %all-reduce.5.cloned.1.call-done, f32[3072]{0:T(1024)S(1)} %bitcast.109), kind=kLoop, calls=%fused_computation.28 | loop fusion | flops 3932160 | bytes 4730880 | tf_op jit(solution)/shard_map/convert_element_type | solution.py:113
  249.0 2.0 collective-permute-start.1
  255.0 13.7 %collective-permute-done.1 = bf16[256,3072]{1,0:T(8,128)(2,1)} collective-permute-done((bf16[256,3072]{1,0:T(8,128)(2,1)}, bf16[256,3072]{1,0:T(8,128)(2,1)}, u32[]{:S(2)}, u32[]{:S(2)}) %collective-permute-start.1) | collective-permute-done | bytes 1572896 | tf_op jit(solution)/shard_map/ppermute | solution.py:16
  268.7 1.8 dynamic-slice_bitcast_fusion
  (61 shorter events, 29.6 us)
Async XLA Ops:
  7.2 65.2 %copy-start = (bf16[1,384,3072]{2,1,0:T(8,128)(2,1)S(1)}, bf16[1,384,3072]{2,1,0:T(8,128)(2,1)}, u32[]{:S(2)}) copy-start(bf16[1,384,3072]{2,1,0:T(8,128)(2,1)} %param.10) | copy-start | bytes 7077892
  7.2 35.6 %all-gather.3.cloned.1.call-start = ((), (), s32[]{:S(2)}) async-start(), calls=%async_computation.2 | async-start | bytes 1966080 | tf_op jit(solution)/shard_map/all_gather | solution.py:99
  7.9 122.4 %all-reduce.3.cloned.1.call-start = ((), (), s32[]{:S(2)}) async-start(), calls=%async_computation | async-start | bytes 3145728 | tf_op jit(solution)/shard_map/psum | solution.py:112
  17.1 10.9 %copy-start.5 = (f32[1,3,3072]{2,0,1:T(1,128)S(1)}, f32[1,3,3072]{2,0,1:T(1,128)}, u32[]{:S(2)}) copy-start(f32[1,3,3072]{2,0,1:T(1,128)} %param.8) | copy-start | bytes 110596
  42.8 3.8 %copy-start.1 = (bf16[1,256,3072]{2,1,0:T(8,128)(2,1)S(1)}, bf16[1,256,3072]{2,1,0:T(8,128)(2,1)}, u32[]{:S(2)}) copy-start(bf16[1,256,3072]{2,1,0:T(8,128)(2,1)} %all-gather.3.cloned.1.call-done) | copy-start | bytes 4718596
  42.8 3.8 %copy-start.6 = (f32[1,1,3072]{2,0,1:T(1,128)S(1)}, f32[1,1,3072]{2,0,1:T(1,128)}, u32[]{:S(2)}) copy-start(f32[1,1,3072]{2,0,1:T(1,128)} %get-tuple-element.9) | copy-start | bytes 36868
  42.8 3.8 %copy-start.8 = (f32[1,1,3072]{2,0,1:T(1,128)S(1)}, f32[1,1,3072]{2,0,1:T(1,128)}, u32[]{:S(2)}) copy-start(f32[1,1,3072]{2,0,1:T(1,128)} %get-tuple-element.10) | copy-start | bytes 36868
  69.3 2.4 copy-start.3
  74.6 170.8 %all-reduce.5.cloned.1.call-start = ((), (), s32[]{:S(2)}) async-start(), calls=%async_computation.1 | async-start | bytes 3145728 | tf_op jit(solution)/shard_map/psum | solution.py:112
  134.0 19.7 %collective-permute-start = (bf16[256,3072]{1,0:T(8,128)(2,1)}, bf16[256,3072]{1,0:T(8,128)(2,1)}, u32[]{:S(2)}, u32[]{:S(2)}) collective-permute-start(bf16[256,3072]{1,0:T(8,128)(2,1)} %fusion.18), channel_id=1, source_target_pairs={{0,4},{4,8},{8,12},{12,16},{16,20},{20,24},{24,28},{28,32},{32,36}... | collective-permute-start | bytes 4718600 | tf_op jit(solution)/shard_map/ppermute | solution.py:16
  136.6 20.7 %copy-start.7 = (f32[1,1,3072]{2,0,1:T(1,128)S(1)}, f32[1,1,3072]{2,0,1:T(1,128)}, u32[]{:S(2)}) copy-start(f32[1,1,3072]{2,0,1:T(1,128)} %get-tuple-element.9) | copy-start | bytes 36868
  136.6 20.7 %copy-start.9 = (f32[1,1,3072]{2,0,1:T(1,128)S(1)}, f32[1,1,3072]{2,0,1:T(1,128)}, u32[]{:S(2)}) copy-start(f32[1,1,3072]{2,0,1:T(1,128)} %get-tuple-element.10) | copy-start | bytes 36868
  163.3 1.1 copy-start.2
  181.0 4.0 %copy-start.4 = (bf16[1152,384]{0,1:T(8,128)(2,1)S(1)}, bf16[1152,384]{0,1:T(8,128)(2,1)}, u32[]{:S(2)}) copy-start(bf16[1152,384]{0,1:T(8,128)(2,1)} %constant_dynamic-update-slice_fusion.1) | copy-start | bytes 2654212
  249.0 19.7 %collective-permute-start.1 = (bf16[256,3072]{1,0:T(8,128)(2,1)}, bf16[256,3072]{1,0:T(8,128)(2,1)}, u32[]{:S(2)}, u32[]{:S(2)}) collective-permute-start(bf16[256,3072]{1,0:T(8,128)(2,1)} %fusion.19), channel_id=1, source_target_pairs={{0,4},{4,8},{8,12},{12,16},{16,20},{20,24},{24,28},{28,32},{32,36}... | collective-permute-start | bytes 4718600 | tf_op jit(solution)/shard_map/ppermute | solution.py:16
Sparse Core Ops, SparseCore 0:
  9.8 32.8 all-gather.2
  74.7 55.5 all-reduce.2
  188.0 57.3 all-reduce.4
where the time goes:
time: 280 us; the launch traced here: 277 us
  waiting for transfers between devices  159 us (57%)
  local copies, waits for them, and re-layouts  47.9 us (17%)
  other arithmetic  28.6 us (10%)
  matrix products  21.8 us (8%)
  between operations  15.9 us (6%)
  starting transfers between devices  4.07 us (1%)
    psum x2, waiting for transfers between devices, per_device(): lax.psum(partial_value.astype(jnp.bfloat16), 'head').astype(jnp.float32)  113 us
    ppermute x2, waiting for transfers between devices, from_behind(): return lax.ppermute(value, axis, pairs)  30.7 us
    unnamed x23, local copies, waits for them, and re-layouts  14.5 us
    all_gather x1, waiting for transfers between devices, per_device(): full_rows = lax.all_gather(own_share, 'head', axis=1, tiled=True)  14.2 us
    dot_general x2, matrix products, project(): projected = jnp.dot(normed, weights, preferred_element_type=jnp.float32)  11.4 us
    convert_element_type x2, other arithmetic, per_device(): (full_rows.astype(jnp.float32) + factors[2] * summed).astype(jnp.bfloat16)  7.3 us
  transfers between devices with their start and end apart: 5, of which 5 were waited for; matrix products, arithmetic and copies ran while one was open for 8% of the time, Pallas kernels for 0%

commit v1 on v0

v1 whole, which is shorter than its diff:
```python
import functools

import jax
import jax.numpy as jnp
from jax import lax
from jax.experimental import pallas as pl
from jax.experimental.pallas import tpu as pltpu
from jax.sharding import PartitionSpec as P

MESH = pl.DeviceIdType.MESH
HEAD_DIM = 128
TICKS = 2
EPSILON = 1e-06
CHUNKS = 4

(
    OWN_RIGHT,
    OWN_LEFT,
    PASS_RIGHT,
    PASS_LEFT,
    FAR_RIGHT,
    FAR_LEFT,
    PLAIN_RIGHT,
    PLAIN_LEFT,
    SUM_RIGHT,
    SUM_LEFT,
    SHIFT,
    KINDS,
) = range(12)


def kernel(
    sections,
    order_ref,
    count_ref,
    state_ref,
    mod_ref,
    wqkv_ref,
    wout_ref,
    stale_ref,
    out_ref,
    fresh_ref,
    rows_buf,
    terms,
    far_buf,
    near_buf,
    y_buf,
    mod,
    wqkv,
    wout,
    stale,
    q_buf,
    k_buf,
    v_buf,
    local_sem,
    send_sem,
    recv_sem,
):
    section = lax.axis_index("section")
    y = lax.axis_index("head")
    ny = 4
    right, left, across = lax.rem(y + 1, ny), lax.rem(y + 3, ny), lax.rem(y + 2, ny)
    behind = lax.rem(section + sections - 1, sections)
    ahead = lax.rem(section + 1, sections)
    to_right, to_left, to_ahead = (section, right), (section, left), (ahead, y)

    patch, share = state_ref.shape
    inner = wout_ref.shape[0]
    heads = inner // HEAD_DIM
    keys = stale_ref.shape[1]
    text = keys - 4 * patch
    width = ny * share
    size = patch // CHUNKS
    half = size // 2

    state_in = pltpu.make_async_copy(state_ref, rows_buf.at[0, y], local_sem.at[0])
    mod_in = pltpu.make_async_copy(mod_ref, mod, local_sem.at[1])
    stale_in = pltpu.make_async_copy(stale_ref, stale, local_sem.at[2])
    wqkv_in = pltpu.make_async_copy(wqkv_ref, wqkv, local_sem.at[3])
    wout_in = pltpu.make_async_copy(wout_ref, wout, local_sem.at[4])
    for copy in (state_in, mod_in, stale_in, wqkv_in, wout_in):
        copy.start()

    barrier = pltpu.get_barrier_semaphore()
    for target in (to_right, to_left, (behind, y)):
        pl.semaphore_signal(barrier, inc=1, device_id=target, device_id_type=MESH)
    pl.semaphore_wait(barrier, 3)

    def rows_of(c, start=0, count=size):
        return pl.ds(pl.multiple_of(c * size + start, 16), count)

    def remote(t, c, kind, source, target, device):
        return pltpu.make_async_remote_copy(
            src_ref=source,
            dst_ref=target,
            send_sem=send_sem.at[t, c, kind],
            recv_sem=recv_sem.at[t, c, kind],
            device_id=device,
            device_id_type=MESH,
        )

    def own_copy(t, c, kind, who, device):
        ref = rows_buf.at[t, who, rows_of(c)]
        return remote(t, c, kind, ref, ref, device)

    def pass_copy(t, c, kind, who, device):
        start = 0 if kind == PASS_RIGHT else half
        ref = rows_buf.at[t, who, rows_of(c, start, half)]
        return remote(t, c, kind, ref, ref, device)

    def far_copy(t, c, kind, who, device):
        side = 0 if kind == FAR_RIGHT else 1
        start = 0 if kind == FAR_RIGHT else half
        return remote(
            t,
            c,
            kind,
            terms.at[t, who, rows_of(c, start, half)],
            far_buf.at[t, side, pl.ds(pl.multiple_of(c * half, 16), half)],
            device,
        )

    def near_copy(t, c, kind, who, device):
        side = 0 if kind in (PLAIN_RIGHT, SUM_RIGHT) else 1
        start = 0 if kind in (SUM_RIGHT, PLAIN_LEFT) else half
        return remote(
            t,
            c,
            kind,
            terms.at[t, who, rows_of(c, start, half)],
            near_buf.at[t, side, rows_of(c, start, half)],
            device,
        )

    def shift_copy(t, c):
        if t + 1 < TICKS:
            target = rows_buf.at[t + 1, y, rows_of(c)]
        else:
            target = out_ref.at[rows_of(c)]
        return remote(t, c, SHIFT, y_buf.at[t, rows_of(c)], target, to_ahead)

    def gather_send(t, c):
        own_copy(t, c, OWN_RIGHT, y, to_right).start()
        own_copy(t, c, OWN_LEFT, y, to_left).start()

    def gather_pass(t, c):
        own_copy(t, c, OWN_RIGHT, left, to_right).wait_recv()
        pass_copy(t, c, PASS_RIGHT, left, to_right).start()
        own_copy(t, c, OWN_LEFT, right, to_left).wait_recv()
        pass_copy(t, c, PASS_LEFT, right, to_left).start()

    def project(t, c):
        pass_copy(t, c, PASS_RIGHT, across, to_right).wait_recv()
        pass_copy(t, c, PASS_LEFT, across, to_left).wait_recv()
        total = jnp.zeros((size, 1), jnp.float32)
        parts = []
        for j in range(ny):
            part = rows_buf[t, j, rows_of(c)].astype(jnp.float32)
            total += jnp.sum(part, axis=-1, keepdims=True)
            parts.append(part)
        centre = total * (1.0 / width)
        spread = jnp.zeros((size, 1), jnp.float32)
        for j in range(ny):
            gap = parts[j] - centre
            spread += jnp.sum(gap * gap, axis=-1, keepdims=True)
        factor = lax.rsqrt(spread * (1.0 / width) + EPSILON)
        sums = [jnp.zeros((size, inner), jnp.float32) for _ in range(3)]
        for j in range(ny):
            columns = slice(j * share, (j + 1) * share)
            part = rows_buf[t, j, rows_of(c)].astype(jnp.float32)
            normed = (part - centre) * factor * (1.0 + mod[1, :, columns]) + mod[0, :, columns]
            normed = normed.astype(jnp.bfloat16)
            for s in range(3):
                sums[s] += jnp.dot(
                    normed, wqkv[s, columns, :], preferred_element_type=jnp.float32
                )
        place = pl.ds(pl.multiple_of(fresh_row(t) + c * size, 16), size)
        for h in range(heads):
            columns = slice(h * HEAD_DIM, (h + 1) * HEAD_DIM)
            for s, target, where in ((0, q_buf, rows_of(c)), (1, k_buf, place)):
                value = sums[s][:, columns]
                square = jnp.mean(value * value, axis=-1, keepdims=True)
                target[where, columns] = (value * lax.rsqrt(square + EPSILON)).astype(jnp.bfloat16)
            v_buf[place, 2 * h * HEAD_DIM : (2 * h + 1) * HEAD_DIM] = sums[2][:, columns].astype(
                jnp.bfloat16
            )

    def fresh_row(t):
        return text + 3 * patch + t * patch

    def attend(t, c):
        window = slice(t * patch, t * patch + keys)
        text_at = patch if t == 0 else 0
        position = lax.broadcasted_iota(jnp.int32, (size, text), 1)
        alive = position < count_ref[0]
        mixed = []
        for h in range(heads):
            columns = slice(h * HEAD_DIM, (h + 1) * HEAD_DIM)
            scores = lax.dot_general(
                q_buf[rows_of(c), columns],
                k_buf[window, columns],
                (((1,), (1,)), ((), ())),
                preferred_element_type=jnp.float32,
            )
            weights = jnp.exp(scores * HEAD_DIM ** (-0.5))
            pieces = [jnp.where(alive, weights[:, text_at : text_at + text], 0.0)]
            if text_at:
                pieces.insert(0, weights[:, :text_at])
            pieces.append(weights[:, text_at + text :])
            weights = jnp.concatenate(pieces, axis=1).astype(jnp.bfloat16)
            both = jnp.dot(
                weights,
                v_buf[window, 2 * h * HEAD_DIM : 2 * (h + 1) * HEAD_DIM],
                preferred_element_type=jnp.float32,
            )
            mixed.append((both[:, :HEAD_DIM] / both[:, HEAD_DIM:]).astype(jnp.bfloat16))
        mixed = jnp.concatenate(mixed, axis=1)
        for j in range(ny):
            columns = slice(j * share, (j + 1) * share)
            terms[t, j, rows_of(c)] = jnp.dot(
                mixed, wout[:, columns], preferred_element_type=jnp.float32
            ).astype(jnp.bfloat16)
        far_copy(t, c, FAR_RIGHT, across, to_right).start()
        far_copy(t, c, FAR_LEFT, across, to_left).start()
        near_copy(t, c, PLAIN_RIGHT, right, to_right).start()
        near_copy(t, c, PLAIN_LEFT, left, to_left).start()

    def combine(t, c):
        for far, near, who, device, side, start in (
            (FAR_RIGHT, SUM_RIGHT, right, to_right, 0, 0),
            (FAR_LEFT, SUM_LEFT, left, to_left, 1, half),
        ):
            far_copy(t, c, far, who, device).wait_recv()
            rows = rows_of(c, start, half)
            arrived = far_buf[t, side, pl.ds(pl.multiple_of(c * half, 16), half)]
            terms[t, who, rows] = (
                terms[t, who, rows].astype(jnp.float32) + arrived.astype(jnp.float32)
            ).astype(jnp.bfloat16)
            near_copy(t, c, near, who, device).start()

    def finish(t, c):
        for kind in (PLAIN_RIGHT, PLAIN_LEFT, SUM_RIGHT, SUM_LEFT):
            device = to_right if kind in (PLAIN_RIGHT, SUM_RIGHT) else to_left
            near_copy(t, c, kind, y, device).wait_recv()
        rows = rows_of(c)
        total = terms[t, y, rows].astype(jnp.float32)
        total += near_buf[t, 0, rows].astype(jnp.float32)
        total += near_buf[t, 1, rows].astype(jnp.float32)
        gate = mod[2, :, pl.ds(pl.multiple_of(y * share, 128), share)]
        y_buf[t, rows] = (rows_buf[t, y, rows].astype(jnp.float32) + gate * total).astype(
            jnp.bfloat16
        )
        shift_copy(t, c).start()

    def arrive(t, c):
        shift_copy(t - 1, c).wait_recv()
        gather_send(t, c)

    def pipeline(stages):
        def step(i, carry):
            for late, stage in enumerate(stages):

                @pl.when(jnp.logical_and(i >= late, i < CHUNKS + late))
                def _():
                    stage(i - late)

            return carry

        lax.fori_loop(0, CHUNKS + len(stages) - 1, step, 0)

    state_in.wait()
    for c in range(CHUNKS):
        gather_send(0, c)
    mod_in.wait()
    stale_in.wait()
    slot = lax.rem(4 * sections - section, 4)
    for place, later in ((0, 1), (patch + text, 2), (2 * patch + text, 3)):
        which = jnp.full((patch, inner), order_ref[lax.rem(slot + later, 4)], jnp.int32)
        picked = [stale[s, text : text + patch].astype(jnp.float32) for s in range(2)]
        for k in range(1, 4):
            source = slice(text + k * patch, text + (k + 1) * patch)
            for s in range(2):
                picked[s] = jnp.where(which == k, stale[s, source].astype(jnp.float32), picked[s])
        k_buf[place : place + patch] = picked[0].astype(jnp.bfloat16)
        for h in range(heads):
            v_buf[place : place + patch, 2 * h * HEAD_DIM : (2 * h + 1) * HEAD_DIM] = picked[1][
                :, h * HEAD_DIM : (h + 1) * HEAD_DIM
            ].astype(jnp.bfloat16)
    k_buf[patch : patch + text] = stale[0, :text]
    for h in range(heads):
        v_buf[patch : patch + text, 2 * h * HEAD_DIM : (2 * h + 1) * HEAD_DIM] = stale[
            1, :text, h * HEAD_DIM : (h + 1) * HEAD_DIM
        ]
        v_buf[:, (2 * h + 1) * HEAD_DIM : 2 * (h + 1) * HEAD_DIM] = jnp.ones(
            (keys + patch, HEAD_DIM), jnp.bfloat16
        )
    wqkv_in.wait()
    wout_in.wait()

    pipeline([functools.partial(gather_pass, 0), functools.partial(project, 0)])
    pipeline(
        [functools.partial(stage, 0) for stage in (attend, combine, finish)]
        + [functools.partial(stage, 1) for stage in (arrive, gather_pass, project)]
    )
    copies = []
    for t in range(TICKS):
        place = slice(fresh_row(t), fresh_row(t) + patch)
        copies.append(
            pltpu.make_async_copy(k_buf.at[place], fresh_ref.at[t, 0], local_sem.at[5 + 4 * t])
        )
        for h in range(heads):
            copies.append(
                pltpu.make_async_copy(
                    v_buf.at[place, 2 * h * HEAD_DIM : (2 * h + 1) * HEAD_DIM],
                    fresh_ref.at[t, 1, :, h * HEAD_DIM : (h + 1) * HEAD_DIM],
                    local_sem.at[6 + 4 * t + h],
                )
            )
    for copy in copies:
        copy.start()
    pipeline([functools.partial(stage, 1) for stage in (attend, combine, finish)])

    for copy in copies:
        copy.wait()

    def drain(c, carry):
        shift_copy(TICKS - 1, c).wait_recv()
        for t in range(TICKS):
            own_copy(t, c, OWN_RIGHT, y, to_right).wait_send()
            own_copy(t, c, OWN_LEFT, y, to_left).wait_send()
            pass_copy(t, c, PASS_RIGHT, left, to_right).wait_send()
            pass_copy(t, c, PASS_LEFT, right, to_left).wait_send()
            far_copy(t, c, FAR_RIGHT, across, to_right).wait_send()
            far_copy(t, c, FAR_LEFT, across, to_left).wait_send()
            near_copy(t, c, PLAIN_RIGHT, right, to_right).wait_send()
            near_copy(t, c, PLAIN_LEFT, left, to_left).wait_send()
            near_copy(t, c, SUM_RIGHT, right, to_right).wait_send()
            near_copy(t, c, SUM_LEFT, left, to_left).wait_send()
            shift_copy(t, c).wait_send()
        return carry

    lax.fori_loop(0, CHUNKS, drain, 0)


def solution(mesh):
    sections = mesh.shape["section"]

    def per_device(state, modulation, w_qkv, w_out, stale_kv, patch_order, text_count):
        patch, share = state.shape[1:]
        width = modulation.shape[2]
        inner = w_out.shape[1]
        keys = stale_kv.shape[2]
        heads = inner // HEAD_DIM
        bf16 = jnp.bfloat16
        anywhere = pl.BlockSpec(memory_space=pl.ANY)
        scalars = pl.BlockSpec(memory_space=pltpu.SMEM)
        flops = TICKS * 2 * patch * inner * (3 * width + 2 * keys + width)
        out, fresh = pl.pallas_call(
            functools.partial(kernel, sections),
            out_shape=(
                jax.ShapeDtypeStruct((patch, share), bf16),
                jax.ShapeDtypeStruct((TICKS, 2, patch, inner), bf16),
            ),
            in_specs=[scalars, scalars] + [anywhere] * 5,
            out_specs=(anywhere, anywhere),
            scratch_shapes=[
                pltpu.VMEM((TICKS, 4, patch, share), bf16),
                pltpu.VMEM((TICKS, 4, patch, share), bf16),
                pltpu.VMEM((TICKS, 2, patch // 2, share), bf16),
                pltpu.VMEM((TICKS, 2, patch, share), bf16),
                pltpu.VMEM((TICKS, patch, share), bf16),
                pltpu.VMEM((3, 1, width), jnp.float32),
                pltpu.VMEM((3, width, inner), bf16),
                pltpu.VMEM((inner, width), bf16),
                pltpu.VMEM((2, keys, inner), bf16),
                pltpu.VMEM((patch, inner), bf16),
                pltpu.VMEM((keys + patch, inner), bf16),
                pltpu.VMEM((keys + patch, 2 * heads * HEAD_DIM), bf16),
                pltpu.SemaphoreType.DMA((16,)),
                pltpu.SemaphoreType.DMA((TICKS, CHUNKS, KINDS)),
                pltpu.SemaphoreType.DMA((TICKS, CHUNKS, KINDS)),
            ],
            compiler_params=pltpu.CompilerParams(
                collective_id=0, has_side_effects=True, vmem_limit_bytes=48 * 2**20
            ),
            cost_estimate=pl.CostEstimate(
                flops=flops, bytes_accessed=14 * 2**20, transcendentals=TICKS * patch * keys * heads
            ),
        )(
            patch_order,
            text_count,
            state[0],
            jnp.transpose(modulation, (1, 0, 2)),
            jnp.transpose(w_qkv[0], (1, 0, 2)),
            w_out[0],
            stale_kv[0],
        )
        return out[None], fresh[None]

    return jax.shard_map(
        per_device,
        mesh=mesh,
        in_specs=(
            P("section", None, "head"),
            P("section", None, None),
            P("section", None, None, "head"),
            P("section", "head", None),
            P("section", None, None, "head"),
            P(),
            P(),
        ),
        out_specs=(P("section", None, "head"), P("section", None, None, None, "head")),
        check_vma=False,
    )
```

time: 280 us -> 90.1 us (0.32)
  waiting for transfers between devices: 159 us -> 0 us
  Pallas kernels: 0 us -> 81 us
  local copies, waits for them, and re-layouts: 47.9 us -> 7.18 us
  other arithmetic: 28.6 us -> 0 us
  matrix products: 21.8 us -> 0 us
  between operations: 15.9 us -> 1.3 us
  starting transfers between devices: 4.07 us -> 0 us
    psum x2 -> x0, waiting for transfers between devices: 113 us -> none  [per_device(): lax.psum(partial_value.astype(jnp.bfloat16), 'head').astype(jnp.float32)]
    pallas_call x0 -> x1, Pallas kernels: none -> 81 us  [per_device(): pl.pallas_call(functools.partial(kernel, sections), out_shape=(jax.ShapeD...]
    ppermute x2 -> x0, waiting for transfers between devices: 30.7 us -> none  [from_behind(): return lax.ppermute(value, axis, pairs)]
    dot_general x8 -> x0, matrix products: 21.8 us -> none  [the longest x2 11.4 us: project(): projected = jnp.dot(normed, weights, preferred_element_type=jnp.float32)]
    all_gather x1 -> x0, waiting for transfers between devices: 14.2 us -> none  [per_device(): full_rows = lax.all_gather(own_share, 'head', axis=1, tiled=True)]
    reduce_sum x8 -> x0, other arithmetic: 11.6 us -> none  [the longest x4 4.14 us: head_norm(): squares = jnp.mean(shaped * shaped, axis=-1, keepdims=True)]
    slice x7 -> x0, local copies, waits for them, and re-layouts: 11.4 us -> none  [the longest x4 4.95 us: project(): new_values = projected[:, 2 * inner_width:].astype(jnp.bfloat16)]
    mul x6 -> x0, local copies, waits for them, and re-layouts: 9.19 us -> none  [the longest x4 5.37 us: head_norm(): return (shaped * lax.rsqrt(squares + epsilon)).astype(jnp.bfloat16)]
  transfers between devices with their start and end apart: 5 -> 0, of which waited for: 5 -> 0; matrix products, arithmetic and copies ran while one was open for 8% -> 0% of each run, Pallas kernels for 0% -> 0%
where the time goes in v1:
time: 90.1 us; the launch traced here: 89.5 us
  Pallas kernels  81 us (90%)
  local copies, waits for them, and re-layouts  7.18 us (8%)
  between operations  1.3 us (1%)
    pallas_call x1, Pallas kernels, per_device(): pl.pallas_call(functools.partial(kernel, sections), out_shape=(jax.ShapeD...  81 us
    unnamed x12, local copies, waits for them, and re-layouts  7.18 us

profile of v1, /device:TPU:1, one launch (start us, length us, event | category | flops | bytes accessed | tf_op | source)
XLA Modules:
  0.0 89.5 jit_solution(9490293211702264296)
XLA Ops:
  1.3 0.0 copy-start
  1.3 1.7 %copy-done = bf16[1,384,3072]{2,1,0:T(8,128)(2,1)S(1)} copy-done((bf16[1,384,3072]{2,1,0:T(8,128)(2,1)S(1)}, bf16[1,384,3072]{2,1,0:T(8,128)(2,1)}, u32[]{:S(2)}) %copy-start) | copy-done | bytes 2359320
  2.9 0.0 copy-start.1
  2.9 1.5 %copy-done.1 = bf16[1,2,1152,384]{3,2,1,0:T(8,128)(2,1)S(1)} copy-done((bf16[1,2,1152,384]{3,2,1,0:T(8,128)(2,1)S(1)}, bf16[1,2,1152,384]{3,2,1,0:T(8,128)(2,1)}, u32[]{:S(2)}) %copy-start.1) | copy-done | bytes 1769496
  4.4 0.0 copy-start.2
  4.4 1.0 %copy-done.2 = bf16[1,256,768]{2,1,0:T(8,128)(2,1)S(1)} copy-done((bf16[1,256,768]{2,1,0:T(8,128)(2,1)S(1)}, bf16[1,256,768]{2,1,0:T(8,128)(2,1)}, u32[]{:S(2)}) %copy-start.2) | copy-done | bytes 393240
  5.4 0.0 copy-start.3
  5.4 0.8 copy-done.3
  6.2 0.0 copy-start.4
  6.2 0.7 copy-done.4
  6.8 81.0 %shard_map.86 = (bf16[256,768]{1,0:T(8,128)(2,1)S(1)}, bf16[2,2,256,384]{3,2,1,0:T(8,128)(2,1)S(1)}) custom-call(s32[4]{0:T(128)S(1)} %copy-done.4, s32[1]{0:T(128)S(6)} %copy.11.count_ref, bf16[256,768]{1,0:T(8,128)(2,1)S(1)} %bitcast.13, f32[3,1,3072]{2,1,0:T(1,128)S(1)} %bitcast.14, bf16[3,3072,384]{2,1,0:T(8,128)(2,1)} %bitcast.15, ...), custom_call_target="tpu_custom_call" | custom-call | flops 5737807872 | bytes 14680064 | tf_op jit(solution)/shard_map/pallas_call | solution.py:358
  87.8 0.7 copy.12
  88.6 0.9 copy.13
Async XLA Ops:
  1.3 1.7 %copy-start = (bf16[1,384,3072]{2,1,0:T(8,128)(2,1)S(1)}, bf16[1,384,3072]{2,1,0:T(8,128)(2,1)}, u32[]{:S(2)}) copy-start(bf16[1,384,3072]{2,1,0:T(8,128)(2,1)} %param.10) | copy-start | bytes 7077892
  2.9 1.5 %copy-start.1 = (bf16[1,2,1152,384]{3,2,1,0:T(8,128)(2,1)S(1)}, bf16[1,2,1152,384]{3,2,1,0:T(8,128)(2,1)}, u32[]{:S(2)}) copy-start(bf16[1,2,1152,384]{3,2,1,0:T(8,128)(2,1)} %param.11) | copy-start | bytes 5308420
  4.4 1.0 %copy-start.2 = (bf16[1,256,768]{2,1,0:T(8,128)(2,1)S(1)}, bf16[1,256,768]{2,1,0:T(8,128)(2,1)}, u32[]{:S(2)}) copy-start(bf16[1,256,768]{2,1,0:T(8,128)(2,1)} %param.7) | copy-start | bytes 1179652
  5.4 0.8 copy-start.3
  6.2 0.7 copy-start.4

commit v2 on v1

v2 whole, which is shorter than its diff:
```python
import functools

import jax
import jax.numpy as jnp
from jax import lax
from jax.experimental import pallas as pl
from jax.experimental.pallas import tpu as pltpu
from jax.sharding import PartitionSpec as P

MESH = pl.DeviceIdType.MESH
HEAD_DIM = 128
TICKS = 2
EPSILON = 1e-06
SPANS = ((0, 128), (128, 128))

(
    OWN_RIGHT,
    OWN_LEFT,
    PASS_RIGHT,
    PASS_LEFT,
    FAR_RIGHT,
    FAR_LEFT,
    PLAIN_RIGHT,
    PLAIN_LEFT,
    SUM_RIGHT,
    SUM_LEFT,
    SHIFT,
    KINDS,
) = range(12)


def spans_of(patch):
    return [(start * patch // 256, size * patch // 256) for start, size in SPANS]


def kernel(
    sections,
    order_ref,
    count_ref,
    state_ref,
    mod_ref,
    wqkv_ref,
    wout_ref,
    stale_ref,
    out_ref,
    fresh_ref,
    rows_buf,
    terms,
    far_buf,
    near_buf,
    y_buf,
    mod,
    wqkv,
    wout,
    stale,
    h_buf,
    q_buf,
    k_buf,
    v_buf,
    local_sem,
    send_sem,
    recv_sem,
    go_sem,
):
    section = lax.axis_index("section")
    y = lax.axis_index("head")
    ny = 4
    right, left, across = lax.rem(y + 1, ny), lax.rem(y + 3, ny), lax.rem(y + 2, ny)
    behind = lax.rem(section + sections - 1, sections)
    ahead = lax.rem(section + 1, sections)
    to_right, to_left, to_ahead = (section, right), (section, left), (ahead, y)

    patch, share = state_ref.shape
    inner = wout_ref.shape[0]
    heads = inner // HEAD_DIM
    keys = stale_ref.shape[1]
    text = keys - 4 * patch
    width = ny * share
    spans = spans_of(patch)
    chunks = len(spans)

    loads = [
        (state_ref, rows_buf.at[0, y]),
        (stale_ref, stale),
        (mod_ref, mod),
    ]
    for s in range(3):
        loads.append((wqkv_ref.at[s], wqkv.at[:, s * inner : (s + 1) * inner]))
    loads.append((wout_ref, wout))
    loads = [
        pltpu.make_async_copy(source, target, local_sem.at[i])
        for i, (source, target) in enumerate(loads)
    ]
    for load in loads:
        load.start()

    barrier = pltpu.get_barrier_semaphore()
    for target in (to_right, to_left, (behind, y)):
        pl.semaphore_signal(barrier, inc=1, device_id=target, device_id_type=MESH)
    pl.semaphore_wait(barrier, 3)

    def rows_of(c):
        start, size = spans[c]
        return slice(start, start + size)

    def half_of(c, second):
        start, size = spans[c]
        start += second * (size // 2)
        return slice(start, start + size // 2)

    def remote(t, c, kind, source, target, device):
        return pltpu.make_async_remote_copy(
            src_ref=source,
            dst_ref=target,
            send_sem=send_sem.at[t, c, kind],
            recv_sem=recv_sem.at[t, c, kind],
            device_id=device,
            device_id_type=MESH,
        )

    def own_copy(t, c, kind, who, device):
        ref = rows_buf.at[t, who, rows_of(c)]
        return remote(t, c, kind, ref, ref, device)

    def pass_copy(t, c, kind, who, device):
        ref = rows_buf.at[t, who, half_of(c, kind == PASS_LEFT)]
        return remote(t, c, kind, ref, ref, device)

    def far_copy(t, c, kind, who, device):
        rows = half_of(c, kind == FAR_LEFT)
        return remote(t, c, kind, terms.at[t, who, rows], far_buf.at[t, rows], device)

    def near_copy(t, c, kind, who, device):
        side = 0 if kind in (PLAIN_RIGHT, SUM_RIGHT) else 1
        rows = half_of(c, kind in (PLAIN_RIGHT, SUM_LEFT))
        return remote(t, c, kind, terms.at[t, who, rows], near_buf.at[t, side, rows], device)

    def shift_copy(t, c):
        if t + 1 < TICKS:
            target = rows_buf.at[t + 1, y, rows_of(c)]
        else:
            target = out_ref.at[rows_of(c)]
        return remote(t, c, SHIFT, y_buf.at[t, rows_of(c)], target, to_ahead)

    def gather_send(t, c):
        own_copy(t, c, OWN_RIGHT, y, to_right).start()
        own_copy(t, c, OWN_LEFT, y, to_left).start()

    def gather_pass(t, c):
        own_copy(t, c, OWN_RIGHT, left, to_right).wait_recv()
        pass_copy(t, c, PASS_RIGHT, left, to_right).start()
        own_copy(t, c, OWN_LEFT, right, to_left).wait_recv()
        pass_copy(t, c, PASS_LEFT, right, to_left).start()

    def project(t, c):
        pass_copy(t, c, PASS_RIGHT, across, to_right).wait_recv()
        pass_copy(t, c, PASS_LEFT, across, to_left).wait_recv()
        start, size = spans[c]
        rows = rows_of(c)
        centre = mean_of([rows_buf[t, j, rows].astype(jnp.float32) for j in range(ny)])
        squares = []
        for j in range(ny):
            gap = rows_buf[t, j, rows].astype(jnp.float32) - centre
            squares.append(gap * gap)
        factor = lax.rsqrt(mean_of(squares) + EPSILON)
        for j in range(ny):
            columns = slice(j * share, (j + 1) * share)
            gap = rows_buf[t, j, rows].astype(jnp.float32) - centre
            normed = gap * factor * (1.0 + mod[1, :, columns]) + mod[0, :, columns]
            h_buf[rows, columns] = normed.astype(jnp.bfloat16)
        sums = jnp.dot(h_buf[rows], wqkv[...], preferred_element_type=jnp.float32)
        place = slice(fresh_row(t) + start, fresh_row(t) + start + size)
        for h in range(heads):
            columns = slice(h * HEAD_DIM, (h + 1) * HEAD_DIM)
            q_buf[rows, columns] = head_norm(sums[:, columns])
            fresh_key = head_norm(sums[:, inner + h * HEAD_DIM : inner + (h + 1) * HEAD_DIM])
            k_buf[place, columns] = fresh_key
            fresh_ref[t, 0, rows, columns] = fresh_key
            first = 2 * inner + h * HEAD_DIM
            fresh_value = sums[:, first : first + HEAD_DIM].astype(jnp.bfloat16)
            v_buf[place, 2 * h * HEAD_DIM : (2 * h + 1) * HEAD_DIM] = fresh_value
            fresh_ref[t, 1, rows, columns] = fresh_value

    def mean_of(parts):
        folded = None
        for part in parts:
            for k in range(share // HEAD_DIM):
                piece = part[:, k * HEAD_DIM : (k + 1) * HEAD_DIM]
                folded = piece if folded is None else folded + piece
        return jnp.sum(folded, axis=-1, keepdims=True) * (1.0 / width)

    def head_norm(value):
        square = jnp.mean(value * value, axis=-1, keepdims=True)
        return (value * lax.rsqrt(square + EPSILON)).astype(jnp.bfloat16)

    def fresh_row(t):
        return text + 3 * patch + t * patch

    def attend(t, c):
        size = spans[c][1]
        window = slice(t * patch, t * patch + keys)
        text_at = patch if t == 0 else 0
        position = lax.broadcasted_iota(jnp.int32, (size, text), 1)
        alive = position < count_ref[0]
        mixed = []
        for h in range(heads):
            columns = slice(h * HEAD_DIM, (h + 1) * HEAD_DIM)
            scores = lax.dot_general(
                q_buf[rows_of(c), columns],
                k_buf[window, columns],
                (((1,), (1,)), ((), ())),
                preferred_element_type=jnp.float32,
            )
            weights = jnp.exp(scores * HEAD_DIM ** (-0.5))
            pieces = [jnp.where(alive, weights[:, text_at : text_at + text], 0.0)]
            if text_at:
                pieces.insert(0, weights[:, :text_at])
            pieces.append(weights[:, text_at + text :])
            weights = jnp.concatenate(pieces, axis=1).astype(jnp.bfloat16)
            both = jnp.dot(
                weights,
                v_buf[window, 2 * h * HEAD_DIM : 2 * (h + 1) * HEAD_DIM],
                preferred_element_type=jnp.float32,
            )
            mixed.append((both[:, :HEAD_DIM] / both[:, HEAD_DIM:]).astype(jnp.bfloat16))
        mixed = jnp.concatenate(mixed, axis=1)
        for j in range(ny):
            columns = slice(j * share, (j + 1) * share)
            terms[t, j, rows_of(c)] = jnp.dot(
                mixed, wout[:, columns], preferred_element_type=jnp.float32
            ).astype(jnp.bfloat16)
        far_copy(t, c, FAR_RIGHT, across, to_right).start()
        far_copy(t, c, FAR_LEFT, across, to_left).start()

    def plain(t, c):
        near_copy(t, c, PLAIN_RIGHT, right, to_right).start()
        near_copy(t, c, PLAIN_LEFT, left, to_left).start()

    def combine(t, c):
        for far, near, who, device in (
            (FAR_RIGHT, SUM_RIGHT, right, to_right),
            (FAR_LEFT, SUM_LEFT, left, to_left),
        ):
            far_copy(t, c, far, who, device).wait_recv()
            rows = half_of(c, far == FAR_LEFT)
            terms[t, who, rows] = (
                terms[t, who, rows].astype(jnp.float32) + far_buf[t, rows].astype(jnp.float32)
            ).astype(jnp.bfloat16)
            near_copy(t, c, near, who, device).start()

    def finish(t, c):
        for kind in (PLAIN_RIGHT, PLAIN_LEFT, SUM_RIGHT, SUM_LEFT):
            device = to_right if kind in (PLAIN_RIGHT, SUM_RIGHT) else to_left
            near_copy(t, c, kind, y, device).wait_recv()
        rows = rows_of(c)
        total = terms[t, y, rows].astype(jnp.float32)
        total += near_buf[t, 0, rows].astype(jnp.float32)
        total += near_buf[t, 1, rows].astype(jnp.float32)
        gate = mod[2, :, pl.ds(pl.multiple_of(y * share, 128), share)]
        y_buf[t, rows] = (rows_buf[t, y, rows].astype(jnp.float32) + gate * total).astype(
            jnp.bfloat16
        )
        shift_copy(t, c).start()

    def arrive(t, c):
        shift_copy(t - 1, c).wait_recv()
        gather_send(t, c)

    first_core = lax.rem(section, 2) == 0
    loads[0].wait()

    @pl.when(first_core)
    def _():
        for c in range(chunks):
            gather_send(0, c)

    for load in loads[1:2]:
        load.wait()
    slot = lax.rem(4 * sections - section, 4)
    for place, later in ((0, 1), (patch + text, 2), (2 * patch + text, 3)):
        which = jnp.full((patch, inner), order_ref[lax.rem(slot + later, 4)], jnp.int32)
        picked = [stale[s, text : text + patch].astype(jnp.float32) for s in range(2)]
        for k in range(1, 4):
            source = slice(text + k * patch, text + (k + 1) * patch)
            for s in range(2):
                picked[s] = jnp.where(which == k, stale[s, source].astype(jnp.float32), picked[s])
        k_buf[place : place + patch] = picked[0].astype(jnp.bfloat16)
        for h in range(heads):
            v_buf[place : place + patch, 2 * h * HEAD_DIM : (2 * h + 1) * HEAD_DIM] = picked[1][
                :, h * HEAD_DIM : (h + 1) * HEAD_DIM
            ].astype(jnp.bfloat16)
    k_buf[patch : patch + text] = stale[0, :text]
    for h in range(heads):
        v_buf[patch : patch + text, 2 * h * HEAD_DIM : (2 * h + 1) * HEAD_DIM] = stale[
            1, :text, h * HEAD_DIM : (h + 1) * HEAD_DIM
        ]
        v_buf[:, (2 * h + 1) * HEAD_DIM : 2 * (h + 1) * HEAD_DIM] = jnp.ones(
            (keys + patch, HEAD_DIM), jnp.bfloat16
        )

    @pl.when(jnp.logical_not(first_core))
    def _():
        pl.semaphore_wait(go_sem, 1)
        for c in range(chunks):
            gather_send(0, c)

    for t in range(TICKS):
        if t:
            for c in range(chunks):
                arrive(t, c)
        for c in range(chunks):
            gather_pass(t, c)
            if t == 0 and c == 0:

                @pl.when(first_core)
                def _():
                    pl.semaphore_signal(go_sem, inc=1, device_id=to_ahead, device_id_type=MESH)

        if t == 0:
            for load in loads[2:]:
                load.wait()
        for stage in (project, attend, plain, combine, finish):
            for c in range(chunks):
                stage(t, c)

    for c in range(chunks):
        shift_copy(TICKS - 1, c).wait_recv()
        for t in range(TICKS):
            own_copy(t, c, OWN_RIGHT, y, to_right).wait_send()
            own_copy(t, c, OWN_LEFT, y, to_left).wait_send()
            pass_copy(t, c, PASS_RIGHT, left, to_right).wait_send()
            pass_copy(t, c, PASS_LEFT, right, to_left).wait_send()
            far_copy(t, c, FAR_RIGHT, across, to_right).wait_send()
            far_copy(t, c, FAR_LEFT, across, to_left).wait_send()
            near_copy(t, c, PLAIN_RIGHT, right, to_right).wait_send()
            near_copy(t, c, PLAIN_LEFT, left, to_left).wait_send()
            near_copy(t, c, SUM_RIGHT, right, to_right).wait_send()
            near_copy(t, c, SUM_LEFT, left, to_left).wait_send()
            shift_copy(t, c).wait_send()


def solution(mesh):
    sections = mesh.shape["section"]

    def per_device(state, modulation, w_qkv, w_out, stale_kv, patch_order, text_count):
        patch, share = state.shape[1:]
        width = modulation.shape[2]
        inner = w_out.shape[1]
        keys = stale_kv.shape[2]
        heads = inner // HEAD_DIM
        bf16 = jnp.bfloat16
        anywhere = pl.BlockSpec(memory_space=pl.ANY)
        chunks = len(spans_of(patch))
        flops = TICKS * 2 * patch * inner * (3 * width + 2 * keys + width)
        out, fresh = pl.pallas_call(
            functools.partial(kernel, sections),
            out_shape=(
                pltpu.VMEM((patch, share), bf16),
                pltpu.VMEM((TICKS, 2, patch, inner), bf16),
            ),
            in_specs=[pl.BlockSpec(memory_space=pltpu.SMEM)] * 2 + [anywhere] * 5,
            out_specs=(pl.BlockSpec(memory_space=pltpu.VMEM),) * 2,
            scratch_shapes=[
                pltpu.VMEM((TICKS, 4, patch, share), bf16),
                pltpu.VMEM((TICKS, 4, patch, share), bf16),
                pltpu.VMEM((TICKS, patch, share), bf16),
                pltpu.VMEM((TICKS, 2, patch, share), bf16),
                pltpu.VMEM((TICKS, patch, share), bf16),
                pltpu.VMEM((3, 1, width), jnp.float32),
                pltpu.VMEM((width, 3 * inner), bf16),
                pltpu.VMEM((inner, width), bf16),
                pltpu.VMEM((2, keys, inner), bf16),
                pltpu.VMEM((patch, width), bf16),
                pltpu.VMEM((patch, inner), bf16),
                pltpu.VMEM((keys + patch, inner), bf16),
                pltpu.VMEM((keys + patch, 2 * heads * HEAD_DIM), bf16),
                pltpu.SemaphoreType.DMA((16,)),
                pltpu.SemaphoreType.DMA((TICKS, chunks, KINDS)),
                pltpu.SemaphoreType.DMA((TICKS, chunks, KINDS)),
                pltpu.SemaphoreType.REGULAR,
            ],
            compiler_params=pltpu.CompilerParams(
                collective_id=0, has_side_effects=True, vmem_limit_bytes=48 * 2**20
            ),
            cost_estimate=pl.CostEstimate(
                flops=flops, bytes_accessed=14 * 2**20, transcendentals=TICKS * patch * keys * heads
            ),
        )(
            pltpu.with_memory_space_constraint(patch_order, pltpu.HBM),
            text_count,
            *(
                pltpu.with_memory_space_constraint(value, pltpu.HBM)
                for value in (
                    state[0],
                    jnp.transpose(modulation, (1, 0, 2)),
                    jnp.transpose(w_qkv[0], (1, 0, 2)),
                    w_out[0],
                    stale_kv[0],
                )
            ),
        )
        return out[None], fresh[None]

    return jax.shard_map(
        per_device,
        mesh=mesh,
        in_specs=(
            P("section", None, "head"),
            P("section", None, None),
            P("section", None, None, "head"),
            P("section", "head", None),
            P("section", None, None, "head"),
            P(),
            P(),
        ),
        out_specs=(P("section", None, "head"), P("section", None, None, None, "head")),
        check_vma=False,
    )
```

time: 90.1 us -> 77.5 us (0.86)
  Pallas kernels: 81 us -> 74.5 us
  local copies, waits for them, and re-layouts: 7.18 us -> 1.63 us
    pallas_call x1, Pallas kernels: 81 us -> 74.5 us  [per_device(): pl.pallas_call(functools.partial(kernel, sections), out_shape=(pltpu.VMEM...]
    unnamed x12 -> x2, local copies, waits for them, and re-layouts: 7.18 us -> 1.63 us
where the time goes in v2:
time: 77.5 us; the launch traced here: 77.4 us
  Pallas kernels  74.5 us (96%)
  local copies, waits for them, and re-layouts  1.63 us (2%)
  between operations  1.29 us (2%)
    pallas_call x1, Pallas kernels, per_device(): pl.pallas_call(functools.partial(kernel, sections), out_shape=(pltpu.VMEM...  74.5 us
    unnamed x2, local copies, waits for them, and re-layouts  1.63 us

profile of v2, /device:TPU:1, one launch (start us, length us, event | category | flops | bytes accessed | tf_op | source)
XLA Modules:
  0.0 77.4 jit_solution(11495919238754183391)
XLA Ops:
  1.3 74.5 %shard_map.86 = (bf16[256,768]{1,0:T(8,128)(2,1)S(1)}, bf16[2,2,256,384]{3,2,1,0:T(8,128)(2,1)S(1)}) custom-call(s32[4]{0:T(128)} %order_ref.1, s32[1]{0:T(128)S(6)} %copy.13.count_ref, bf16[256,768]{1,0:T(8,128)(2,1)} %bitcast.14, f32[3,1,3072]{2,1,0:T(1,128)} %bitcast.15, bf16[3,3072,384]{2,1,0:T(8,128)(2,1)} %bitcast.11, bf16[384,3072]{1,0:T(8,128)(2,1)} %bitcast.12, ...), custom_call_target="tpu_custom_call" | custom-call | flops 5737807872 | bytes 14680064 | tf_op jit(solution)/shard_map/pallas_call | solution.py:355
  75.8 0.7 copy.11
  76.5 0.9 %copy.12 = bf16[1,2,2,256,384]{4,3,2,1,0:T(8,128)(2,1)} copy(bf16[1,2,2,256,384]{4,3,2,1,0:T(8,128)(2,1)S(1)} %bitcast.9) | data formatting | bytes 1572864

commit v3 on v2

--- a/solution.py
+++ b/solution.py
@@ -11,7 +11,9 @@
 HEAD_DIM = 128
 TICKS = 2
 EPSILON = 1e-06
-SPANS = ((0, 128), (128, 128))
+SPANS = ((0, 64), (64, 64), (128, 64), (192, 64))
+GROUPS = ((0, 1), (2, 3))
+
 
 (
     OWN_RIGHT,
@@ -54,6 +56,7 @@
     wout,
     stale,
     h_buf,
+    early,
     q_buf,
     k_buf,
     v_buf,
@@ -152,11 +155,16 @@
         own_copy(t, c, OWN_LEFT, right, to_left).wait_recv()
         pass_copy(t, c, PASS_LEFT, right, to_left).start()
 
-    def project(t, c):
-        pass_copy(t, c, PASS_RIGHT, across, to_right).wait_recv()
-        pass_copy(t, c, PASS_LEFT, across, to_left).wait_recv()
-        start, size = spans[c]
-        rows = rows_of(c)
+    def group_rows(g):
+        start = spans[GROUPS[g][0]][0]
+        return start, sum(spans[c][1] for c in GROUPS[g])
+
+    def project(t, g):
+        for c in GROUPS[g]:
+            pass_copy(t, c, PASS_RIGHT, across, to_right).wait_recv()
+            pass_copy(t, c, PASS_LEFT, across, to_left).wait_recv()
+        start, size = group_rows(g)
+        rows = slice(start, start + size)
         centre = mean_of([rows_buf[t, j, rows].astype(jnp.float32) for j in range(ny)])
         squares = []
         for j in range(ny):
@@ -196,41 +204,58 @@
     def fresh_row(t):
         return text + 3 * patch + t * patch
 
-    def attend(t, c):
-        size = spans[c][1]
-        window = slice(t * patch, t * patch + keys)
+    def attention(t, g, h, first, last):
+        start, size = group_rows(g)
+        columns = slice(h * HEAD_DIM, (h + 1) * HEAD_DIM)
+        window = slice(t * patch + first, t * patch + last)
+        scores = lax.dot_general(
+            q_buf[start : start + size, columns],
+            k_buf[window, columns],
+            (((1,), (1,)), ((), ())),
+            preferred_element_type=jnp.float32,
+        )
+        weights = jnp.exp(scores * HEAD_DIM ** (-0.5))
         text_at = patch if t == 0 else 0
-        position = lax.broadcasted_iota(jnp.int32, (size, text), 1)
-        alive = position < count_ref[0]
-        mixed = []
-        for h in range(heads):
-            columns = slice(h * HEAD_DIM, (h + 1) * HEAD_DIM)
-            scores = lax.dot_general(
-                q_buf[rows_of(c), columns],
-                k_buf[window, columns],
-                (((1,), (1,)), ((), ())),
-                preferred_element_type=jnp.float32,
-            )
-            weights = jnp.exp(scores * HEAD_DIM ** (-0.5))
+        if first <= text_at < last:
+            position = lax.broadcasted_iota(jnp.int32, (size, text), 1)
+            alive = position < count_ref[0]
             pieces = [jnp.where(alive, weights[:, text_at : text_at + text], 0.0)]
             if text_at:
                 pieces.insert(0, weights[:, :text_at])
             pieces.append(weights[:, text_at + text :])
-            weights = jnp.concatenate(pieces, axis=1).astype(jnp.bfloat16)
-            both = jnp.dot(
-                weights,
-                v_buf[window, 2 * h * HEAD_DIM : 2 * (h + 1) * HEAD_DIM],
-                preferred_element_type=jnp.float32,
-            )
+            weights = jnp.concatenate(pieces, axis=1)
+        return jnp.dot(
+            weights.astype(jnp.bfloat16),
+            v_buf[window, 2 * h * HEAD_DIM : 2 * (h + 1) * HEAD_DIM],
+            preferred_element_type=jnp.float32,
+        )
+
+    known = keys - group_rows(len(GROUPS) - 1)[1]
+
+    def attend_early(t, g):
+        start, size = group_rows(g)
+        for h in range(heads):
+            early[h, start : start + size] = attention(t, g, h, 0, known)
+
+    def attend(t, g):
+        start, size = group_rows(g)
+        rows = slice(start, start + size)
+        mixed = []
+        for h in range(heads):
+            if g < len(GROUPS) - 1:
+                both = early[h, rows] + attention(t, g, h, known, keys)
+            else:
+                both = attention(t, g, h, 0, keys)
             mixed.append((both[:, :HEAD_DIM] / both[:, HEAD_DIM:]).astype(jnp.bfloat16))
         mixed = jnp.concatenate(mixed, axis=1)
         for j in range(ny):
             columns = slice(j * share, (j + 1) * share)
-            terms[t, j, rows_of(c)] = jnp.dot(
+            terms[t, j, rows] = jnp.dot(
                 mixed, wout[:, columns], preferred_element_type=jnp.float32
             ).astype(jnp.bfloat16)
-        far_copy(t, c, FAR_RIGHT, across, to_right).start()
-        far_copy(t, c, FAR_LEFT, across, to_left).start()
+        for c in GROUPS[g]:
+            far_copy(t, c, FAR_RIGHT, across, to_right).start()
+            far_copy(t, c, FAR_LEFT, across, to_left).start()
 
     def plain(t, c):
         near_copy(t, c, PLAIN_RIGHT, right, to_right).start()
@@ -304,11 +329,9 @@
         for c in range(chunks):
             gather_send(0, c)
 
+    everything = range(chunks)
     for t in range(TICKS):
-        if t:
-            for c in range(chunks):
-                arrive(t, c)
-        for c in range(chunks):
+        for c in everything:
             gather_pass(t, c)
             if t == 0 and c == 0:
 
@@ -316,12 +339,46 @@
                 def _():
                     pl.semaphore_signal(go_sem, inc=1, device_id=to_ahead, device_id_type=MESH)
 
+        if t == 1:
+
+            @pl.when(lax.rem(section, sections // 4) == 0)
+            def _():
+                pl.semaphore_signal(go_sem, inc=1, device_id=to_ahead, device_id_type=MESH)
+
         if t == 0:
             for load in loads[2:]:
                 load.wait()
-        for stage in (project, attend, plain, combine, finish):
-            for c in range(chunks):
-                stage(t, c)
+        for g in range(len(GROUPS)):
+            project(t, g)
+            if g < len(GROUPS) - 1:
+                attend_early(t, g)
+        if t == 1:
+
+            @pl.when(lax.rem(section, sections // 4) == 1)
+            def _():
+                pl.semaphore_wait(go_sem, 1)
+
+        for g in range(len(GROUPS)):
+            attend(t, g)
+        for c in everything:
+            plain(t, c)
+        for c in everything:
+            combine(t, c)
+        if t + 1 < TICKS:
+
+            @pl.when(jnp.logical_not(first_core))
+            def _():
+                for c in everything:
+                    arrive(t + 1, c)
+
+        for c in everything:
+            finish(t, c)
+        if t + 1 < TICKS:
+
+            @pl.when(first_core)
+            def _():
+                for c in everything:
+                    arrive(t + 1, c)
 
     for c in range(chunks):
         shift_copy(TICKS - 1, c).wait_recv()
@@ -371,6 +428,7 @@
                 pltpu.VMEM((inner, width), bf16),
                 pltpu.VMEM((2, keys, inner), bf16),
                 pltpu.VMEM((patch, width), bf16),
+                pltpu.VMEM((heads, patch, 2 * HEAD_DIM), jnp.float32),
                 pltpu.VMEM((patch, inner), bf16),
                 pltpu.VMEM((keys + patch, inner), bf16),
                 pltpu.VMEM((keys + patch, 2 * heads * HEAD_DIM), bf16),

time: 77.5 us -> 74.3 us (0.959)
  Pallas kernels: 74.5 us -> 71.3 us
    pallas_call x1, Pallas kernels: 74.5 us -> 71.3 us  [per_device(): pl.pallas_call(functools.partial(kernel, sections), out_shape=(pltpu.VMEM...]
where the time goes in v3:
time: 74.3 us; the launch traced here: 74.2 us
  Pallas kernels  71.3 us (96%)
  local copies, waits for them, and re-layouts  1.63 us (2%)
  between operations  1.29 us (2%)
    pallas_call x1, Pallas kernels, per_device(): pl.pallas_call(functools.partial(kernel, sections), out_shape=(pltpu.VMEM...  71.3 us
    unnamed x2, local copies, waits for them, and re-layouts  1.63 us

profile of v3, /device:TPU:1, one launch (start us, length us, event | category | flops | bytes accessed | tf_op | source)
XLA Modules:
  0.0 74.2 jit_solution(2074364041342149780)
XLA Ops:
  1.3 71.3 %shard_map.86 = (bf16[256,768]{1,0:T(8,128)(2,1)S(1)}, bf16[2,2,256,384]{3,2,1,0:T(8,128)(2,1)S(1)}) custom-call(s32[4]{0:T(128)} %order_ref.1, s32[1]{0:T(128)S(6)} %copy.13.count_ref, bf16[256,768]{1,0:T(8,128)(2,1)} %bitcast.14, f32[3,1,3072]{2,1,0:T(1,128)} %bitcast.15, bf16[3,3072,384]{2,1,0:T(8,128)(2,1)} %bitcast.11, bf16[384,3072]{1,0:T(8,128)(2,1)} %bitcast.12, ...), custom_call_target="tpu_custom_call" | custom-call | flops 5737807872 | bytes 14680064 | tf_op jit(solution)/shard_map/pallas_call | solution.py:412
  72.6 0.7 %copy.11 = bf16[1,256,768]{2,1,0:T(8,128)(2,1)} copy(bf16[1,256,768]{2,1,0:T(8,128)(2,1)S(1)} %bitcast.10) | data formatting | bytes 786432
  73.3 0.9 %copy.12 = bf16[1,2,2,256,384]{4,3,2,1,0:T(8,128)(2,1)} copy(bf16[1,2,2,256,384]{4,3,2,1,0:T(8,128)(2,1)S(1)} %bitcast.9) | data formatting | bytes 1572864

commit v4 on v3

--- a/solution.py
+++ b/solution.py
@@ -165,17 +165,16 @@
             pass_copy(t, c, PASS_LEFT, across, to_left).wait_recv()
         start, size = group_rows(g)
         rows = slice(start, start + size)
-        centre = mean_of([rows_buf[t, j, rows].astype(jnp.float32) for j in range(ny)])
-        squares = []
-        for j in range(ny):
-            gap = rows_buf[t, j, rows].astype(jnp.float32) - centre
-            squares.append(gap * gap)
-        factor = lax.rsqrt(mean_of(squares) + EPSILON)
-        for j in range(ny):
-            columns = slice(j * share, (j + 1) * share)
-            gap = rows_buf[t, j, rows].astype(jnp.float32) - centre
-            normed = gap * factor * (1.0 + mod[1, :, columns]) + mod[0, :, columns]
-            h_buf[rows, columns] = normed.astype(jnp.bfloat16)
+        for first in range(start, start + size, 16):
+            few = slice(first, first + 16)
+            parts = [rows_buf[t, j, few].astype(jnp.float32) for j in range(ny)]
+            centre = mean_of(parts)
+            parts = [part - centre for part in parts]
+            factor = lax.rsqrt(mean_of([part * part for part in parts]) + EPSILON)
+            for j in range(ny):
+                columns = slice(j * share, (j + 1) * share)
+                normed = parts[j] * factor * (1.0 + mod[1, :, columns]) + mod[0, :, columns]
+                h_buf[few, columns] = normed.astype(jnp.bfloat16)
         sums = jnp.dot(h_buf[rows], wqkv[...], preferred_element_type=jnp.float32)
         place = slice(fresh_row(t) + start, fresh_row(t) + start + size)
         for h in range(heads):
@@ -256,6 +255,8 @@
         for c in GROUPS[g]:
             far_copy(t, c, FAR_RIGHT, across, to_right).start()
             far_copy(t, c, FAR_LEFT, across, to_left).start()
+        for c in GROUPS[g]:
+            plain(t, c)
 
     def plain(t, c):
         near_copy(t, c, PLAIN_RIGHT, right, to_right).start()
@@ -361,8 +362,6 @@
         for g in range(len(GROUPS)):
             attend(t, g)
         for c in everything:
-            plain(t, c)
-        for c in everything:
             combine(t, c)
         if t + 1 < TICKS:
 
@@ -380,9 +379,8 @@
                 for c in everything:
                     arrive(t + 1, c)
 
-    for c in range(chunks):
-        shift_copy(TICKS - 1, c).wait_recv()
-        for t in range(TICKS):
+    for t in range(TICKS):
+        for c in everything:
             own_copy(t, c, OWN_RIGHT, y, to_right).wait_send()
             own_copy(t, c, OWN_LEFT, y, to_left).wait_send()
             pass_copy(t, c, PASS_RIGHT, left, to_right).wait_send()
@@ -394,6 +392,8 @@
             near_copy(t, c, SUM_RIGHT, right, to_right).wait_send()
             near_copy(t, c, SUM_LEFT, left, to_left).wait_send()
             shift_copy(t, c).wait_send()
+    for c in everything:
+        shift_copy(TICKS - 1, c).wait_recv()
 
 
 def solution(mesh):

time: 74.3 us -> 73.5 us (0.989)
  Pallas kernels: 71.3 us -> 70.5 us
    pallas_call x1, Pallas kernels: 71.3 us -> 70.5 us  [per_device(): pl.pallas_call(functools.partial(kernel, sections), out_shape=(pltpu.VMEM...]
where the time goes in v4:
time: 73.5 us; the launch traced here: 73.4 us
  Pallas kernels  70.5 us (96%)
  local copies, waits for them, and re-layouts  1.63 us (2%)
  between operations  1.29 us (2%)
    pallas_call x1, Pallas kernels, per_device(): pl.pallas_call(functools.partial(kernel, sections), out_shape=(pltpu.VMEM...  70.5 us
    unnamed x2, local copies, waits for them, and re-layouts  1.63 us

profile of v4, /device:TPU:1, one launch (start us, length us, event | category | flops | bytes accessed | tf_op | source)
XLA Modules:
  0.0 73.4 jit_solution(15278065643017373784)
XLA Ops:
  1.3 70.5 %shard_map.86 = (bf16[256,768]{1,0:T(8,128)(2,1)S(1)}, bf16[2,2,256,384]{3,2,1,0:T(8,128)(2,1)S(1)}) custom-call(s32[4]{0:T(128)} %order_ref.1, s32[1]{0:T(128)S(6)} %copy.13.count_ref, bf16[256,768]{1,0:T(8,128)(2,1)} %bitcast.14, f32[3,1,3072]{2,1,0:T(1,128)} %bitcast.15, bf16[3,3072,384]{2,1,0:T(8,128)(2,1)} %bitcast.11, bf16[384,3072]{1,0:T(8,128)(2,1)} %bitcast.12, ...), custom_call_target="tpu_custom_call" | custom-call | flops 5737807872 | bytes 14680064 | tf_op jit(solution)/shard_map/pallas_call | solution.py:412
  71.7 0.7 %copy.11 = bf16[1,256,768]{2,1,0:T(8,128)(2,1)} copy(bf16[1,256,768]{2,1,0:T(8,128)(2,1)S(1)} %bitcast.10) | data formatting | bytes 786432
  72.5 0.9 %copy.12 = bf16[1,2,2,256,384]{4,3,2,1,0:T(8,128)(2,1)} copy(bf16[1,2,2,256,384]{4,3,2,1,0:T(8,128)(2,1)S(1)} %bitcast.9) | data formatting | bytes 1572864

commit v5 on v4

--- a/solution.py
+++ b/solution.py
@@ -123,7 +123,8 @@
 
     def own_copy(t, c, kind, who, device):
         ref = rows_buf.at[t, who, rows_of(c)]
-        return remote(t, c, kind, ref, ref, device)
+        source = state_ref.at[rows_of(c)] if t == 0 else ref
+        return remote(t, c, kind, source, ref, device)
 
     def pass_copy(t, c, kind, who, device):
         ref = rows_buf.at[t, who, half_of(c, kind == PASS_LEFT)]
@@ -293,14 +294,13 @@
         gather_send(t, c)
 
     first_core = lax.rem(section, 2) == 0
-    loads[0].wait()
 
     @pl.when(first_core)
     def _():
         for c in range(chunks):
             gather_send(0, c)
 
-    for load in loads[1:2]:
+    for load in loads[:2]:
         load.wait()
     slot = lax.rem(4 * sections - section, 4)
     for place, later in ((0, 1), (patch + text, 2), (2 * patch + text, 3)):

time: 73.5 us -> 73.7 us (level)
  no operation moved by 1% of the time
where the time goes in v5:
time: 73.7 us; the launch traced here: 73.6 us
  Pallas kernels  70.7 us (96%)
  local copies, waits for them, and re-layouts  1.63 us (2%)
  between operations  1.29 us (2%)
    pallas_call x1, Pallas kernels, per_device(): pl.pallas_call(functools.partial(kernel, sections), out_shape=(pltpu.VMEM...  70.7 us
    unnamed x2, local copies, waits for them, and re-layouts  1.63 us

profile of v5, /device:TPU:1, one launch (start us, length us, event | category | flops | bytes accessed | tf_op | source)
XLA Modules:
  0.0 73.6 jit_solution(10605053887841820125)
XLA Ops:
  1.3 70.7 %shard_map.86 = (bf16[256,768]{1,0:T(8,128)(2,1)S(1)}, bf16[2,2,256,384]{3,2,1,0:T(8,128)(2,1)S(1)}) custom-call(s32[4]{0:T(128)} %order_ref.1, s32[1]{0:T(128)S(6)} %copy.13.count_ref, bf16[256,768]{1,0:T(8,128)(2,1)} %bitcast.14, f32[3,1,3072]{2,1,0:T(1,128)} %bitcast.15, bf16[3,3072,384]{2,1,0:T(8,128)(2,1)} %bitcast.11, bf16[384,3072]{1,0:T(8,128)(2,1)} %bitcast.12, ...), custom_call_target="tpu_custom_call" | custom-call | flops 5737807872 | bytes 14680064 | tf_op jit(solution)/shard_map/pallas_call | solution.py:412
  72.0 0.7 %copy.11 = bf16[1,256,768]{2,1,0:T(8,128)(2,1)} copy(bf16[1,256,768]{2,1,0:T(8,128)(2,1)S(1)} %bitcast.10) | data formatting | bytes 786432
  72.8 0.9 %copy.12 = bf16[1,2,2,256,384]{4,3,2,1,0:T(8,128)(2,1)} copy(bf16[1,2,2,256,384]{4,3,2,1,0:T(8,128)(2,1)S(1)} %bitcast.9) | data formatting | bytes 1572864
